TPU v7x, 32 devices: a whole 2x2x4 slice. The times are simulated.
32 devices in a mesh: dp: 8 (over y, x, core), ctx: 4 (over z).
Axes of the slice: x: 2, y: 2, z: 4, core: 2. Of those that a mesh axis runs over, the one named last changes fastest.
Arguments:
- layer_input: bfloat16 [8, 640, 8192], P('dp', 'ctx'), may hold values from -6 to 6
- query_rows: bfloat16 [8, 640, 1024], P('dp', 'ctx'), may hold values from -8 to 8
- key_rows: bfloat16 [8, 640, 128], P('dp', 'ctx'), may hold values from -8 to 8
- value_rows: bfloat16 [8, 640, 128], P('dp', 'ctx'), may hold values from -6 to 6
- grad_out: bfloat16 [8, 640, 1024], P('dp', 'ctx'), may hold values from -6 to 6
- doc_lengths: int32 [8, 8], P('dp'), may hold values from 1 to 320, 640 in all within a row
- block_order: int32 [8], replicated, may hold values from 0 to 7, each once
Outputs:
- query_grad: bfloat16 [8, 640, 1024], P('dp', 'ctx')
- weight_grad: bfloat16 [8192, 256], P(('dp', 'ctx'))
Inputs may be any that keep to these rules, and one draw needn't show every extreme that they name: `block_order`: each number of 0 to 7 appears once. `doc_lengths`: the lengths of a row sum to 640; the longest of each row is half of 640.
All inputs are finite; a program needn't handle non-finite values.
Results may differ from a plain program's by a relative error of at most 0.01.
Values may be sent and summed in bfloat16 or wider, within the bound.
A program may use at most 64 MiB of HBM per device.

v0:
```python
import jax
import jax.numpy as jnp
from jax import lax
from jax.sharding import PartitionSpec as P


def passed_along(value, axis, steps):
    count = lax.axis_size(axis)
    pairs = [(source, (source + steps) % count) for source in range(count)]
    return lax.ppermute(value, axis, pairs)


def shard_positions(block_order, owner, rows):
    half = rows // 2
    local = jnp.arange(rows, dtype=jnp.int32)
    first = lax.dynamic_index_in_dim(block_order, 2 * owner, 0, keepdims=False)
    second = lax.dynamic_index_in_dim(block_order, 2 * owner + 1, 0, keepdims=False)
    blocks = jnp.where(local < half, first, second)
    return blocks * half + local % half


def document_ids(position, ends):
    return jnp.sum((ends[None, :] <= position[:, None]).astype(jnp.int32), axis=1)


def contract_rows(left, right):
    return lax.dot_general(
        left, right, (((0,), (0,)), ((), ())), preferred_element_type=jnp.float32
    )


def contract_cols(left, right):
    return lax.dot_general(
        left, right, (((1,), (1,)), ((), ())), preferred_element_type=jnp.float32
    )


def per_device(layer_input, query_rows, key_rows, value_rows, grad_out, doc_lengths, block_order):
    rows = query_rows.shape[1]
    width = key_rows.shape[2]
    heads = query_rows.shape[2] // width
    parts = lax.axis_size("ctx")
    me = lax.axis_index("ctx")
    scale = width ** (-0.5)
    ends = jnp.cumsum(doc_lengths[0])
    queries = query_rows[0].reshape(rows * heads, width)
    grads = grad_out[0].reshape(rows * heads, width)
    own_pos = shard_positions(block_order, me, rows)
    query_pos = jnp.repeat(own_pos, heads)
    query_doc = jnp.repeat(document_ids(own_pos, ends), heads)
    paired = jnp.concatenate([key_rows[0], value_rows[0]], axis=1)
    query_zero = jnp.zeros((rows * heads, width), jnp.float32)
    pair_zero = jnp.zeros((rows, 2 * width), jnp.float32)

    def allowed_for(owner):
        key_pos = shard_positions(block_order, owner, rows)
        key_doc = document_ids(key_pos, ends)
        return (query_doc[:, None] == key_doc[None, :]) & (key_pos[None, :] <= query_pos[:, None])

    def forward_terms(state, block, allowed):
        best, total, weighted = state
        scores = contract_cols(queries, block[:, :width]) * scale
        masked = jnp.where(allowed, scores, -jnp.inf)
        new_best = jnp.maximum(best, jnp.max(masked, axis=1))
        safe_best = jnp.where(jnp.isfinite(new_best), new_best, 0.0)
        probs = jnp.where(allowed, jnp.exp(masked - safe_best[:, None]), 0.0)
        dprobs = contract_cols(grads, block[:, width:])
        factor = jnp.exp(best - safe_best)
        return (
            new_best,
            total * factor + jnp.sum(probs, axis=1),
            weighted * factor + jnp.sum(probs * dprobs, axis=1),
        )

    def forward_step(state, block, owner):
        allowed = allowed_for(owner)
        return forward_terms(state, block, allowed)

    def backward_terms(block, allowed, lse, delta):
        scores = contract_cols(queries, block[:, :width]) * scale
        probs = jnp.where(allowed, jnp.exp(scores - lse[:, None]), 0.0)
        dprobs = contract_cols(grads, block[:, width:])
        dscores = (probs * (dprobs - delta[:, None])).astype(jnp.bfloat16)
        weights = probs.astype(jnp.bfloat16)
        dquery = jnp.dot(dscores, block[:, :width], preferred_element_type=jnp.float32)
        dpair = jnp.concatenate(
            [contract_rows(dscores, queries), contract_rows(weights, grads)], axis=1
        )
        return (dquery, dpair)

    def backward_step(block, owner, lse, delta):
        allowed = allowed_for(owner)
        return backward_terms(block, allowed, lse, delta)

    start_state = (
        jnp.full((rows * heads,), -jnp.inf, jnp.float32),
        jnp.zeros((rows * heads,), jnp.float32),
        jnp.zeros((rows * heads,), jnp.float32),
    )

    def forward_turn(turn, carry):
        state, block = carry
        state = forward_step(state, block, (me - turn) % parts)
        block = passed_along(block, "ctx", 1)
        return (state, block)

    state, block = lax.fori_loop(0, parts - 1, forward_turn, (start_state, paired))
    best, total, weighted = forward_step(state, block, (me + 1) % parts)
    lse = best + jnp.log(total)
    delta = weighted / total

    def backward_turn(turn, carry):
        block, pair_grad, dquery = carry
        add_query, add_pair = backward_step(block, (me - turn) % parts, lse, delta)
        pair_grad = passed_along((pair_grad + add_pair).astype(jnp.bfloat16), "ctx", 1).astype(
            jnp.float32
        )
        block = passed_along(block, "ctx", 1)
        return (block, pair_grad, dquery + add_query)

    block, pair_grad, dquery = lax.fori_loop(
        0, parts, backward_turn, (paired, pair_zero, query_zero)
    )
    column = jnp.where(jnp.arange(2 * width) < width, scale, 1.0)
    pair_low = (pair_grad * column[None, :]).astype(jnp.bfloat16)
    inputs = layer_input[0]
    summed = lax.psum_scatter(
        contract_rows(inputs, pair_low), ("dp", "ctx"), scatter_dimension=0, tiled=True
    )
    grad_scale = (lax.axis_size("dp") * rows * parts) ** (-0.5)
    weight_grad = (summed * grad_scale).astype(jnp.bfloat16)
    query_grad = (dquery * scale).astype(jnp.bfloat16).reshape(1, rows, heads * width)
    return (query_grad, weight_grad)


def solution(mesh):
    placed = (
        P("dp", "ctx", None),
        P("dp", "ctx", None),
        P("dp", "ctx", None),
        P("dp", "ctx", None),
        P("dp", "ctx", None),
        P("dp", None),
        P(),
    )
    return jax.shard_map(
        per_device,
        mesh=mesh,
        in_specs=placed,
        out_specs=(P("dp", "ctx", None), P(("dp", "ctx"), None)),
        check_vma=False,
    )
```

profile of v0, /device:TPU:0, one launch (start us, length us, event | category | flops | bytes accessed | tf_op | source)
XLA Modules:
  0.0 302.1 jit_solution(13018181731342392056)
XLA Ops:
  7.8 0.9 reduce-window.8
  8.8 1.4 pad_maximum_fusion
  10.2 0.9 copy.20
  11.1 1.5 fusion.42
  12.6 3.1 %multiply_add_fusion.1 = (s32[160]{0:T(256)S(1)}, s32[160]{0:T(256)}) fusion(s32[]{:T(128)} %bitcast.7, s32[]{:T(128)} %bitcast.6, s32[]{:T(128)} %bitcast.5, s32[]{:T(128)} %bitcast.4), kind=kLoop, calls=%fused_computation.72 | loop fusion | flops 2080 | bytes 1296 | tf_op jit(solution)/shard_map/add | solution.py:19
  15.6 1.3 convert_reduce_fusion.2
  19.2 1.1 reshape_squeeze.6
  20.3 1.1 reshape_squeeze.7
  21.4 26.4 %while.44 = (s32[]{:T(128)}, f32[1280]{0:T(1024)S(1)}, f32[1280]{0:T(1024)}, f32[1280]{0:T(1024)S(1)}, bf16[160,256]{1,0:T(8,128)(2,1)S(1)}, /*index=5*/s32[8]{0...) while((s32[]{:T(128)}, f32[1280]{0:T(1024)S(1)}, ...), condition=%wide.region_7.8_spmd.clone, body=%wide.region_2.7_spmd.clone.sunk | while | flops 108768176 | bytes 3910573 | solution.py:107
  21.5 3.1 %collective-permute-start = (bf16[160,256]{1,0:T(8,128)(2,1)S(1)}, bf16[160,256]{1,0:T(8,128)(2,1)S(1)}, u32[]{:S(2)}, u32[]{:S(2)}) collective-permute-start(bf16[160,256]{1,0:T(8,128)(2,1)S(1)} %copy.25), channel_id=1, source_target_pairs={{0,1},{1,2},{2,3},{3,0},{4,5},{5,6},{6,7},{7,4},{8,9},{9,10},{10,1... | collective-permute-start | bytes 245768 | tf_op jit(solution)/shard_map/while/body/eval_jaxpr/ppermute | solution.py:10
  26.3 1.4 fusion.84
  27.7 1.3 fusion.85
  31.2 1.6 collective-permute-start
  34.5 1.4 fusion.84
  35.9 1.3 fusion.85
  39.5 1.6 collective-permute-start
  42.8 1.4 fusion.84
  44.2 1.3 fusion.85
  47.8 1.1 fusion.43
  48.9 1.1 fusion.34
  50.4 51.8 %while.45 = (s32[]{:T(128)}, bf16[160,256]{1,0:T(8,128)(2,1)}, f32[160,256]{1,0:T(8,128)}, f32[1280,128]{1,0:T(8,128)}, s32[8]{0:T(128)S(1)}, /*index=5*/s32[]{:...) while((s32[]{:T(128)}, bf16[160,256]{1,0:T(8,128)(2,1)}, ...), condition=%wide.region_14.15_spmd.clone, body=%wide.region_12.14_spmd.clone.sunk | while | flops 264729776 | bytes 8793793 | solution.py:121
  50.4 0.9 copy.36
  53.0 1.3 fusion.101
  56.3 1.8 collective-permute-start.2
  58.0 1.3 convolution_add_fusion.2
  59.3 3.4 %collective-permute-done.2 = bf16[160,256]{1,0:T(8,128)(2,1)S(1)} collective-permute-done((bf16[160,256]{1,0:T(8,128)(2,1)}, bf16[160,256]{1,0:T(8,128)(2,1)S(1)}, u32[]{:S(2)}, u32[]{:S(2)}) %collective-permute-start.2) | collective-permute-done | bytes 81952 | tf_op jit(solution)/shard_map/while/body/eval_jaxpr/ppermute | solution.py:10
  63.4 0.9 copy.36
  66.0 1.3 fusion.101
  69.2 1.5 collective-permute-start.2
  70.7 2.4 convolution_add_fusion.2
  73.1 2.5 collective-permute-done.2
  76.3 0.9 copy.36
  78.9 1.3 fusion.101
  82.1 1.3 collective-permute-start.2
  83.4 2.4 convolution_add_fusion.2
  85.8 2.8 collective-permute-done.2
  89.3 0.9 copy.36
  90.2 0.7 le.359
  91.8 1.3 fusion.101
  95.1 1.5 collective-permute-start.2
  96.6 2.4 convolution_add_fusion.2
  99.0 2.5 collective-permute-done.2
  102.2 5.4 %convolution_bitcast_fusion = f32[8192,256]{0,1:T(8,128)} fusion(bf16[1,160,8192]{2,1,0:T(8,128)(2,1)S(1)} %copy-done, f32[160,256]{1,0:T(8,128)} %get-tuple-element.685, f32[256]{0:T(256)S(1)} %copy-done.14), kind=kOutput, calls=%fused_computation.45 | convolution fusion | flops 671170560 | bytes 11174912 | tf_op jit(solution)/shard_map/dot_general | solution.py:27
  107.7 1.1 multiply_convert_fusion
  108.8 0.9 reshape.142
  109.7 183.8 %reduce-scatter.2.cloned.1.call-done = f32[256,256]{0,1:T(8,128)} async-done(((f32[8192,256]{0,1:T(8,128)}), f32[256,256]{0,1:T(8,128)}) %reduce-scatter.2.cloned.1.call-update) | async-done | bytes 262160 | tf_op jit(solution)/shard_map/reduce_scatter | solution.py:127
  293.5 1.0 multiply_convert_fusion.1
  294.4 0.8 copy.13
  (155 shorter events, 31.2 us)
Async XLA Ops:
  7.2 95.0 %copy-start = (bf16[1,160,8192]{2,1,0:T(8,128)(2,1)S(1)}, bf16[1,160,8192]{2,1,0:T(8,128)(2,1)}, u32[]{:S(2)}) copy-start(bf16[1,160,8192]{2,1,0:T(8,128)(2,1)} %param.11) | copy-start | bytes 7864324
  7.2 286.3 %reduce-scatter.2.cloned.1.call-start = ((), (), s32[]{:S(2)}) async-start(), calls=%async_computation.1 | async-start | bytes 8650752 | tf_op jit(solution)/shard_map/reduce_scatter | solution.py:127
  8.8 8.2 %copy-start.8 = (s32[8,1]{0,1:T(1,128)}, s32[8,1]{0,1:T(1,128)S(1)}, u32[]{:S(2)}) copy-start(s32[8,1]{0,1:T(1,128)S(1)} %reduce-window.8) | copy-start | bytes 100
  15.6 1.3 copy-start.12
  17.0 1.5 copy-start.6
  21.5 9.2 %collective-permute-start = (bf16[160,256]{1,0:T(8,128)(2,1)S(1)}, bf16[160,256]{1,0:T(8,128)(2,1)S(1)}, u32[]{:S(2)}, u32[]{:S(2)}) collective-permute-start(bf16[160,256]{1,0:T(8,128)(2,1)S(1)} %copy.25), channel_id=1, source_target_pairs={{0,1},{1,2},{2,3},{3,0},{4,5},{5,6},{6,7},{7,4},{8,9},{9,10},{10,1... | collective-permute-start | bytes 245768 | tf_op jit(solution)/shard_map/while/body/eval_jaxpr/ppermute | solution.py:10
  26.2 4.4 %copy-start.3 = (f32[1280]{0:T(1024)S(1)}, f32[1280]{0:T(1024)}, u32[]{:S(2)}) copy-start(f32[1280]{0:T(1024)} %get-tuple-element.1054) | copy-start | bytes 15364 | tf_op jit(solution)/shard_map/while
  30.6 0.6 copy-start.4
  31.2 7.7 %collective-permute-start = (bf16[160,256]{1,0:T(8,128)(2,1)S(1)}, bf16[160,256]{1,0:T(8,128)(2,1)S(1)}, u32[]{:S(2)}, u32[]{:S(2)}) collective-permute-start(bf16[160,256]{1,0:T(8,128)(2,1)S(1)} %copy.25), channel_id=1, source_target_pairs={{0,1},{1,2},{2,3},{3,0},{4,5},{5,6},{6,7},{7,4},{8,9},{9,10},{10,1... | collective-permute-start | bytes 245768 | tf_op jit(solution)/shard_map/while/body/eval_jaxpr/ppermute | solution.py:10
  34.5 4.4 %copy-start.3 = (f32[1280]{0:T(1024)S(1)}, f32[1280]{0:T(1024)}, u32[]{:S(2)}) copy-start(f32[1280]{0:T(1024)} %get-tuple-element.1054) | copy-start | bytes 15364 | tf_op jit(solution)/shard_map/while
  38.9 0.6 copy-start.4
  39.5 7.7 %collective-permute-start = (bf16[160,256]{1,0:T(8,128)(2,1)S(1)}, bf16[160,256]{1,0:T(8,128)(2,1)S(1)}, u32[]{:S(2)}, u32[]{:S(2)}) collective-permute-start(bf16[160,256]{1,0:T(8,128)(2,1)S(1)} %copy.25), channel_id=1, source_target_pairs={{0,1},{1,2},{2,3},{3,0},{4,5},{5,6},{6,7},{7,4},{8,9},{9,10},{10,1... | collective-permute-start | bytes 245768 | tf_op jit(solution)/shard_map/while/body/eval_jaxpr/ppermute | solution.py:10
  42.8 4.4 %copy-start.3 = (f32[1280]{0:T(1024)S(1)}, f32[1280]{0:T(1024)}, u32[]{:S(2)}) copy-start(f32[1280]{0:T(1024)} %get-tuple-element.1054) | copy-start | bytes 15364 | tf_op jit(solution)/shard_map/while
  47.2 0.6 copy-start.4
  47.8 2.3 copy-start.10
  47.8 2.3 copy-start.11
  47.8 2.3 copy-start.13
  47.8 2.3 copy-start.15
  47.8 2.5 copy-start.5
  47.8 2.6 copy-start.2
  47.8 2.6 copy-start.7
  47.8 2.6 copy-start.9
  50.4 51.8 %copy-start.14 = (f32[256]{0:T(256)S(1)}, f32[256]{0:T(256)}, u32[]{:S(2)}) copy-start(f32[256]{0:T(256)} %compare_select_fusion.2) | copy-start | bytes 3076
  51.3 12.1 %collective-permute-start.1 = (bf16[160,256]{1,0:T(8,128)(2,1)S(1)}, bf16[160,256]{1,0:T(8,128)(2,1)}, u32[]{:S(2)}, u32[]{:S(2)}) collective-permute-start(bf16[160,256]{1,0:T(8,128)(2,1)S(1)} %copy.36), channel_id=1, source_target_pairs={{0,1},{1,2},{2,3},{3,0},{4,5},{5,6},{6,7},{7,4},{8,9},{9,10},{10,1... | collective-permute-start | bytes 245768 | tf_op jit(solution)/shard_map/while/body/eval_jaxpr/ppermute | solution.py:10
  54.4 1.2 copy-start.1
  56.3 6.4 %collective-permute-start.2 = (bf16[160,256]{1,0:T(8,128)(2,1)}, bf16[160,256]{1,0:T(8,128)(2,1)S(1)}, u32[]{:S(2)}, u32[]{:S(2)}) collective-permute-start(bf16[160,256]{1,0:T(8,128)(2,1)} %fusion.106), channel_id=1, source_target_pairs={{0,1},{1,2},{2,3},{3,0},{4,5},{5,6},{6,7},{7,4},{8,9},{9,10},{10,1... | collective-permute-start | bytes 245768 | tf_op jit(solution)/shard_map/while/body/eval_jaxpr/ppermute | solution.py:10
  64.3 12.0 %collective-permute-start.1 = (bf16[160,256]{1,0:T(8,128)(2,1)S(1)}, bf16[160,256]{1,0:T(8,128)(2,1)}, u32[]{:S(2)}, u32[]{:S(2)}) collective-permute-start(bf16[160,256]{1,0:T(8,128)(2,1)S(1)} %copy.36), channel_id=1, source_target_pairs={{0,1},{1,2},{2,3},{3,0},{4,5},{5,6},{6,7},{7,4},{8,9},{9,10},{10,1... | collective-permute-start | bytes 245768 | tf_op jit(solution)/shard_map/while/body/eval_jaxpr/ppermute | solution.py:10
  67.3 1.2 copy-start.1
  69.2 6.4 %collective-permute-start.2 = (bf16[160,256]{1,0:T(8,128)(2,1)}, bf16[160,256]{1,0:T(8,128)(2,1)S(1)}, u32[]{:S(2)}, u32[]{:S(2)}) collective-permute-start(bf16[160,256]{1,0:T(8,128)(2,1)} %fusion.106), channel_id=1, source_target_pairs={{0,1},{1,2},{2,3},{3,0},{4,5},{5,6},{6,7},{7,4},{8,9},{9,10},{10,1... | collective-permute-start | bytes 245768 | tf_op jit(solution)/shard_map/while/body/eval_jaxpr/ppermute | solution.py:10
  77.2 12.0 %collective-permute-start.1 = (bf16[160,256]{1,0:T(8,128)(2,1)S(1)}, bf16[160,256]{1,0:T(8,128)(2,1)}, u32[]{:S(2)}, u32[]{:S(2)}) collective-permute-start(bf16[160,256]{1,0:T(8,128)(2,1)S(1)} %copy.36), channel_id=1, source_target_pairs={{0,1},{1,2},{2,3},{3,0},{4,5},{5,6},{6,7},{7,4},{8,9},{9,10},{10,1... | collective-permute-start | bytes 245768 | tf_op jit(solution)/shard_map/while/body/eval_jaxpr/ppermute | solution.py:10
  80.3 1.2 copy-start.1
  82.1 6.4 %collective-permute-start.2 = (bf16[160,256]{1,0:T(8,128)(2,1)}, bf16[160,256]{1,0:T(8,128)(2,1)S(1)}, u32[]{:S(2)}, u32[]{:S(2)}) collective-permute-start(bf16[160,256]{1,0:T(8,128)(2,1)} %fusion.106), channel_id=1, source_target_pairs={{0,1},{1,2},{2,3},{3,0},{4,5},{5,6},{6,7},{7,4},{8,9},{9,10},{10,1... | collective-permute-start | bytes 245768 | tf_op jit(solution)/shard_map/while/body/eval_jaxpr/ppermute | solution.py:10
  90.2 12.0 %collective-permute-start.1 = (bf16[160,256]{1,0:T(8,128)(2,1)S(1)}, bf16[160,256]{1,0:T(8,128)(2,1)}, u32[]{:S(2)}, u32[]{:S(2)}) collective-permute-start(bf16[160,256]{1,0:T(8,128)(2,1)S(1)} %copy.36), channel_id=1, source_target_pairs={{0,1},{1,2},{2,3},{3,0},{4,5},{5,6},{6,7},{7,4},{8,9},{9,10},{10,1... | collective-permute-start | bytes 245768 | tf_op jit(solution)/shard_map/while/body/eval_jaxpr/ppermute | solution.py:10
  93.2 1.2 copy-start.1
  95.1 6.4 %collective-permute-start.2 = (bf16[160,256]{1,0:T(8,128)(2,1)}, bf16[160,256]{1,0:T(8,128)(2,1)S(1)}, u32[]{:S(2)}, u32[]{:S(2)}) collective-permute-start(bf16[160,256]{1,0:T(8,128)(2,1)} %fusion.106), channel_id=1, source_target_pairs={{0,1},{1,2},{2,3},{3,0},{4,5},{5,6},{6,7},{7,4},{8,9},{9,10},{10,1... | collective-permute-start | bytes 245768 | tf_op jit(solution)/shard_map/while/body/eval_jaxpr/ppermute | solution.py:10
Sparse Core Ops, SparseCore 0:
  107.8 185.6 reduce-scatter.1
where the time goes:
time: 303 us; the launch traced here: 302 us
  waiting for transfers between devices  195 us (64%)
  local copies, waits for them, and re-layouts  29.5 us (10%)
  other arithmetic  27.2 us (9%)
  matrix products  22.8 us (8%)
  between operations  14.2 us (5%)
  starting transfers between devices  12.4 us (4%)
    reduce_scatter x1, waiting for transfers between devices, per_device(): lax.psum_scatter(contract_rows(inputs, pair_low), ('dp', 'ctx'), scatter_...  184 us
    ppermute x11, starting transfers between devices, passed_along(): return lax.ppermute(value, axis, pairs)  12.4 us
    add x8, other arithmetic, shard_positions(): return blocks * half + local % half  11.9 us
    ppermute x11, waiting for transfers between devices, passed_along(): return lax.ppermute(value, axis, pairs)  11.3 us
    dot_general x4, matrix products, backward_terms(): jnp.dot(dscores, block[:, :width], preferred_element_type=jnp.float32)  8.42 us
    dynamic_slice x8, local copies, waits for them, and re-layouts, shard_positions(): first = lax.dynamic_index_in_dim(block_order, 2 * owner, 0, keepdims=False)  8.01 us
    dot_general x9, matrix products, contract_rows(): lax.dot_general(left, right, (((0,), (0,)), ((), ())), preferred_element_...  7.52 us
    dot_general x16, matrix products, contract_cols(): lax.dot_general(left, right, (((1,), (1,)), ((), ())), preferred_element_...  6.88 us
  transfers between devices with their start and end apart: 12, of which 5 were waited for; matrix products, arithmetic and copies ran while one was open for 17% of the time, Pallas kernels for 0%

commit v1 on v0

--- a/solution.py
+++ b/solution.py
@@ -1,6 +1,10 @@
+import math
+
 import jax
 import jax.numpy as jnp
 from jax import lax
+from jax.experimental import pallas as pl
+from jax.experimental.pallas import tpu as pltpu
 from jax.sharding import PartitionSpec as P
 
 
@@ -23,6 +27,11 @@
     return jnp.sum((ends[None, :] <= position[:, None]).astype(jnp.int32), axis=1)
 
 
+def document_ends(lengths):
+    index = jnp.arange(lengths.shape[0])
+    return jnp.sum(jnp.where(index[None, :] <= index[:, None], lengths[None, :], 0), axis=1)
+
+
 def contract_rows(left, right):
     return lax.dot_general(
         left, right, (((0,), (0,)), ((), ())), preferred_element_type=jnp.float32
@@ -35,14 +44,14 @@
     )
 
 
-def per_device(layer_input, query_rows, key_rows, value_rows, grad_out, doc_lengths, block_order):
+def by_rings(layer_input, query_rows, key_rows, value_rows, grad_out, doc_lengths, block_order):
     rows = query_rows.shape[1]
     width = key_rows.shape[2]
     heads = query_rows.shape[2] // width
     parts = lax.axis_size("ctx")
     me = lax.axis_index("ctx")
     scale = width ** (-0.5)
-    ends = jnp.cumsum(doc_lengths[0])
+    ends = document_ends(doc_lengths[0])
     queries = query_rows[0].reshape(rows * heads, width)
     grads = grad_out[0].reshape(rows * heads, width)
     own_pos = shard_positions(block_order, me, rows)
@@ -133,6 +142,292 @@
     return (query_grad, weight_grad)
 
 
+def kernel(
+    grad_scale, x_ref, q_ref, k_ref, v_ref, g_ref, len_ref, order_ref, dq_ref, dw_ref,
+    qs, gs, kbuf, vbuf, probs, dprobs, dscores, part, landed, pair, xa, xb,
+    early, cross, crossed, zsum, zout, zland,
+    k_send, k_recv, v_send, v_recv, x_send, x_recv, own_sem, part_send, part_recv,
+    pair_send, pair_recv, cross_send, cross_recv, z_send, z_recv,
+):
+    rows, width = k_ref.shape
+    heads = q_ref.shape[1] // width
+    half = rows // 2
+    lanes = rows * heads
+    chunk = dw_ref.shape[0]
+    parts = 4
+    dp, me = lax.axis_index("dp"), lax.axis_index("ctx")
+    y, x, c = dp // 4, (dp // 2) % 2, dp % 2
+
+    def place(yy, xx, cc):
+        return (yy * 2 + xx) * 2 + cc
+
+    def remote(source, target, send, recv, where):
+        return pltpu.make_async_remote_copy(
+            src_ref=source, dst_ref=target, send_sem=send, recv_sem=recv,
+            device_id=where, device_id_type=pl.DeviceIdType.MESH,
+        )
+
+    peers = [(dp, (me + s) % parts) for s in range(1, parts)]
+    near = [
+        (y, x, 1 - c), (y, 1 - x, c), (y, 1 - x, 1 - c), (1 - y, x, c), (1 - y, x, 1 - c),
+    ]
+    close = [(place(*n), me) for n in near]
+
+    barrier = pltpu.get_barrier_semaphore()
+    for where in peers + close:
+        pl.semaphore_signal(barrier, inc=1, device_id=where, device_id_type=pl.DeviceIdType.MESH)
+
+    for h in range(heads):
+        qs[h * rows:(h + 1) * rows, :] = q_ref[:, h * width:(h + 1) * width]
+        gs[h * rows:(h + 1) * rows, :] = g_ref[:, h * width:(h + 1) * width]
+    kbuf[0] = k_ref[...]
+    vbuf[0] = v_ref[...]
+
+    pl.semaphore_wait(barrier, len(peers) + len(close))
+
+    sent, kcopies, vcopies = [], [None], [None]
+    for s in range(1, parts):
+        where = peers[s - 1]
+        kcopies.append(remote(k_ref, kbuf.at[s], k_send.at[s], k_recv.at[s], where))
+        vcopies.append(remote(v_ref, vbuf.at[s], v_send.at[s], v_recv.at[s], where))
+    for s in (2, 1, 3):
+        kcopies[s].start()
+    for s in (2, 1, 3):
+        vcopies[s].start()
+    sent += kcopies[1:] + vcopies[1:]
+
+    xcopies, owned = [], []
+    for slot, (cx, cc) in enumerate([(x, c), (x, 1 - c), (1 - x, c), (1 - x, 1 - c)]):
+        for t in range(2):
+            first = pl.multiple_of(place(t, cx, cc) * (parts * chunk), parts * chunk)
+            source = x_ref.at[:, pl.ds(first, 2 * chunk)]
+            target = xa.at[t, pl.ds(slot * rows, rows), :]
+            if slot == 0:
+                owned.append(pltpu.make_async_copy(source, target, own_sem.at[t]))
+            else:
+                n = slot * 2 + t
+                xcopies.append(remote(source, target, x_send.at[0, n], x_recv.at[0, n], (place(y, cx, cc), me)))
+    for slot, (cy, cc) in enumerate([(y, c), (y, 1 - c), (1 - y, c), (1 - y, 1 - c)]):
+        for t in range(2):
+            first = pl.multiple_of(place(cy, t, cc) * (parts * chunk) + 2 * chunk, 2 * chunk)
+            source = x_ref.at[:, pl.ds(first, 2 * chunk)]
+            target = xb.at[t, pl.ds(slot * rows, rows), :]
+            if slot == 0:
+                owned.append(pltpu.make_async_copy(source, target, own_sem.at[2 + t]))
+            else:
+                n = slot * 2 + t
+                xcopies.append(remote(source, target, x_send.at[1, n], x_recv.at[1, n], (place(cy, x, cc), me)))
+    for copy in xcopies + owned:
+        copy.start()
+    sent += xcopies
+
+    lane = lax.broadcasted_iota(jnp.int32, (1, lanes), 1)
+    inside = lane
+    for h in range(1, heads):
+        inside = inside - jnp.where(lane >= h * rows, rows, 0)
+    first = (order_ref[2 * me]) * half
+    second = (order_ref[2 * me + 1] - 1) * half
+    qpos = inside + jnp.where(inside < half, first, second)
+    begin = jnp.zeros((1, lanes), jnp.int32)
+    end = jnp.int32(0)
+    for j in range(len_ref.shape[1]):
+        end = end + len_ref[0, j]
+        begin = jnp.where(qpos >= end, end, begin)
+    row = lax.broadcasted_iota(jnp.int32, (rows, 1), 0)
+
+    def nt(left, right):
+        return lax.dot_general(left, right, (((1,), (1,)), ((), ())), preferred_element_type=jnp.float32)
+
+    def nn(left, right):
+        return jnp.dot(left, right, preferred_element_type=jnp.float32)
+
+    scale = width ** (-0.5)
+    base2 = scale * math.log2(math.e)
+    order = (0, 1, 3, 2)
+    best = None
+    for s in order:
+        if s:
+            kcopies[s].wait_recv()
+        owner = (me - s + parts) % parts
+        one = (order_ref[2 * owner]) * half
+        two = (order_ref[2 * owner + 1] - 1) * half
+        kpos = row + jnp.where(row < half, one, two)
+        allowed = (kpos >= begin) & (kpos <= qpos)
+        scores = jnp.where(allowed, nt(kbuf[s], qs[...]) * base2, -1e30)
+        probs[s] = scores
+        top = jnp.max(scores, axis=0, keepdims=True)
+        best = top if best is None else jnp.maximum(best, top)
+    total, weighted = 0.0, 0.0
+    for s in order:
+        if s:
+            vcopies[s].wait_recv()
+        prob = jnp.exp2(probs[s] - best)
+        dprob = nt(vbuf[s], gs[...])
+        probs[s] = prob
+        dprobs[s] = dprob
+        total = total + jnp.sum(prob, axis=0, keepdims=True)
+        weighted = weighted + jnp.sum(prob * dprob, axis=0, keepdims=True)
+    inverse = 1.0 / total
+    delta = weighted * inverse
+
+    partcopies = [None]
+    for s in range(1, parts):
+        where = (dp, (me - s + parts) % parts)
+        partcopies.append(remote(part.at[s], landed.at[s], part_send.at[s], part_recv.at[s], where))
+    own_pair = None
+    for s in (2, 1, 3, 0):
+        prob = probs[s] * inverse
+        dscore = (prob * (dprobs[s] - delta)).astype(jnp.bfloat16)
+        dscores[s * rows:(s + 1) * rows, :] = dscore
+        dkey = nn(dscore, qs[...])
+        dvalue = nn(prob.astype(jnp.bfloat16), gs[...])
+        if s:
+            part[s, :, :width] = dkey.astype(jnp.bfloat16)
+            part[s, :, width:] = dvalue.astype(jnp.bfloat16)
+            partcopies[s].start()
+        else:
+            own_pair = (dkey, dvalue)
+    sent += partcopies[1:]
+
+    keys = kbuf[...].reshape(parts * rows, width)
+    dquery = nn(keys.T, dscores[...]) * scale
+    for h in range(heads):
+        dq_ref[:, h * width:(h + 1) * width] = (
+            dquery[:, h * rows:(h + 1) * rows].T.astype(jnp.bfloat16)
+        )
+
+    dkey, dvalue = own_pair
+    for s in (1, 3, 2):
+        partcopies[s].wait_recv()
+        dkey = dkey + landed[s, :, :width].astype(jnp.float32)
+        dvalue = dvalue + landed[s, :, width:].astype(jnp.float32)
+    pair[0:rows, :width] = (dkey * scale).astype(jnp.bfloat16)
+    pair[0:rows, width:] = dvalue.astype(jnp.bfloat16)
+    paircopies = [None]
+    for n in range(1, 6):
+        copy = remote(
+            pair.at[pl.ds(0, rows), :], pair.at[pl.ds(n * rows, rows), :],
+            pair_send.at[n], pair_recv.at[n], close[n - 1],
+        )
+        paircopies.append(copy)
+    for n in (3, 5, 2, 4, 1):
+        paircopies[n].start()
+    sent += paircopies[1:]
+
+    for copy in owned:
+        copy.wait()
+    for copy in xcopies:
+        copy.wait_recv()
+    paircopies[1].wait_recv()
+    turned = pair[0:2 * rows, :].T
+    for t in range(2):
+        early[0, t] = nn(turned, xa[t, 0:2 * rows, :])
+        early[1, t] = nn(turned, xb[t, 0:2 * rows, :])
+    crosscopies = [[], []]
+    kept = (y, x)
+    away = [(place(1 - y, x, c), me), (place(y, 1 - x, c), me)]
+    for a in range(2):
+        for z in range(2):
+            crosscopies[a].append(remote(
+                cross.at[a, z], crossed.at[a, z], cross_send.at[a, z], cross_recv.at[a, z], away[a],
+            ))
+    turns = []
+    for a, xs in enumerate((xa, xb)):
+        paircopies[2 + 2 * a].wait_recv()
+        paircopies[3 + 2 * a].wait_recv()
+        turned = pair[(2 + 2 * a) * rows:(4 + 2 * a) * rows, :].T
+        turns.append(turned)
+        other = 1 - kept[a]
+        for z in range(2):
+            cols = slice(z * chunk, (z + 1) * chunk)
+            made = early[a, other, :, cols] + nn(turned, xs[other, 2 * rows:4 * rows, cols])
+            cross[a, z] = made.astype(jnp.bfloat16)
+            crosscopies[a][z].start()
+    for a, xs in enumerate((xa, xb)):
+        for z in range(2):
+            cols = slice(z * chunk, (z + 1) * chunk)
+            zsum[2 * a + z] = early[a, kept[a], :, cols] + nn(turns[a], xs[kept[a], 2 * rows:4 * rows, cols])
+        sent += crosscopies[a]
+
+    for z, a in ((0, 0), (1, 0), (0, 1), (1, 1)):
+        t = 2 * a + z
+        crosscopies[a][z].wait_recv()
+        made = zsum[t] + crossed[a, z].astype(jnp.float32)
+        zsum[t] = made
+        zout[t] = made.astype(jnp.bfloat16)
+
+        @pl.when(me != t)
+        def _():
+            s = (t - me + parts) % parts
+            remote(zout.at[t], zland.at[s], z_send.at[s], z_recv.at[s], (dp, t)).start()
+
+    final = zsum[me]
+    for s in (1, 3, 2):
+        to = (me + s) % parts
+        copy = remote(zout.at[to], zland.at[s], z_send.at[s], z_recv.at[s], (dp, to))
+        copy.wait_recv()
+        final = final + zland[s].astype(jnp.float32)
+        sent.append(copy)
+    dw_ref[...] = (final * grad_scale).T.astype(jnp.bfloat16)
+    for copy in sent:
+        copy.wait_send()
+
+
+def fused(layer_input, query_rows, key_rows, value_rows, grad_out, doc_lengths, block_order):
+    rows, width = key_rows.shape[1:]
+    model = layer_input.shape[2]
+    heads = query_rows.shape[2] // width
+    count, parts = lax.axis_size("dp"), lax.axis_size("ctx")
+    chunk = model // (count * parts)
+    lanes = rows * heads
+    grad_scale = (count * rows * parts) ** (-0.5)
+    low, full = jnp.bfloat16, jnp.float32
+    vmem = pl.BlockSpec(memory_space=pltpu.VMEM)
+    smem = pl.BlockSpec(memory_space=pltpu.SMEM)
+    dma = pltpu.SemaphoreType.DMA
+
+    def body(*refs):
+        kernel(grad_scale, *refs)
+
+    query_grad, weight_grad = pl.pallas_call(
+        body,
+        out_shape=(
+            jax.ShapeDtypeStruct((rows, heads * width), low),
+            jax.ShapeDtypeStruct((chunk, 2 * width), low),
+        ),
+        in_specs=[pl.BlockSpec(memory_space=pl.ANY), vmem, vmem, vmem, vmem, smem, smem],
+        out_specs=(vmem, vmem),
+        scratch_shapes=[
+            pltpu.VMEM((lanes, width), low),
+            pltpu.VMEM((lanes, width), low),
+            pltpu.VMEM((parts, rows, width), low),
+            pltpu.VMEM((parts, rows, width), low),
+            pltpu.VMEM((parts, rows, lanes), full),
+            pltpu.VMEM((parts, rows, lanes), full),
+            pltpu.VMEM((parts * rows, lanes), low),
+            pltpu.VMEM((parts, rows, 2 * width), low),
+            pltpu.VMEM((parts, rows, 2 * width), low),
+            pltpu.VMEM((6 * rows, 2 * width), low),
+            pltpu.VMEM((2, 4 * rows, 2 * chunk), low),
+            pltpu.VMEM((2, 4 * rows, 2 * chunk), low),
+            pltpu.VMEM((2, 2, 2 * width, 2 * chunk), full),
+            pltpu.VMEM((2, 2, 2 * width, chunk), low),
+            pltpu.VMEM((2, 2, 2 * width, chunk), low),
+            pltpu.VMEM((4, 2 * width, chunk), full),
+            pltpu.VMEM((4, 2 * width, chunk), low),
+            pltpu.VMEM((4, 2 * width, chunk), low),
+            dma((4,)), dma((4,)), dma((4,)), dma((4,)),
+            dma((2, 8)), dma((2, 8)), dma((4,)),
+            dma((4,)), dma((4,)), dma((6,)), dma((6,)),
+            dma((2, 2)), dma((2, 2)), dma((4,)), dma((4,)),
+        ],
+        compiler_params=pltpu.CompilerParams(
+            collective_id=0, has_side_effects=True, vmem_limit_bytes=48 * 1024 * 1024
+        ),
+    )(layer_input[0], query_rows[0], key_rows[0], value_rows[0], grad_out[0], doc_lengths, block_order)
+    return (query_grad[None], weight_grad)
+
+
 def solution(mesh):
     placed = (
         P("dp", "ctx", None),
@@ -144,7 +439,7 @@
         P(),
     )
     return jax.shard_map(
-        per_device,
+        fused if dict(mesh.shape) == {"dp": 8, "ctx": 4} else by_rings,
         mesh=mesh,
         in_specs=placed,
         out_specs=(P("dp", "ctx", None), P(("dp", "ctx"), None)),

time: 303 us -> 53.8 us (0.18)
  the two profiles are of different devices: /device:TPU:0 before, /device:TPU:24 now
where the time goes in v1:
time: 53.8 us; the launch traced here: 53.4 us
  Pallas kernels  44.8 us (83%)
  local copies, waits for them, and re-layouts  7.92 us (15%)
  between operations  0.66 us (1%)
    pallas_call x1, Pallas kernels, fused(): pl.pallas_call(body, out_shape=(jax.ShapeDtypeStruct((rows, heads * width...  44.8 us
    unnamed x16, local copies, waits for them, and re-layouts  7.92 us

profile of v1, /device:TPU:24, one launch (start us, length us, event | category | flops | bytes accessed | tf_op | source)
XLA Modules:
  0.0 53.4 jit_solution(862903585326326173)
XLA Ops:
  0.6 0.0 copy-start
  0.6 1.7 %copy-done = bf16[1,160,8192]{2,1,0:T(8,128)(2,1)S(1)} copy-done((bf16[1,160,8192]{2,1,0:T(8,128)(2,1)S(1)}, bf16[1,160,8192]{2,1,0:T(8,128)(2,1)}, u32[]{:S(2)}) %copy-start) | copy-done | bytes 2621464
  2.4 0.0 copy-start.1
  2.4 1.0 %copy-done.1 = bf16[1,160,1024]{2,1,0:T(8,128)(2,1)S(1)} copy-done((bf16[1,160,1024]{2,1,0:T(8,128)(2,1)S(1)}, bf16[1,160,1024]{2,1,0:T(8,128)(2,1)}, u32[]{:S(2)}) %copy-start.1) | copy-done | bytes 327704
  3.3 0.0 copy-start.2
  3.3 1.0 %copy-done.2 = bf16[1,160,1024]{2,1,0:T(8,128)(2,1)S(1)} copy-done((bf16[1,160,1024]{2,1,0:T(8,128)(2,1)S(1)}, bf16[1,160,1024]{2,1,0:T(8,128)(2,1)}, u32[]{:S(2)}) %copy-start.2) | copy-done | bytes 327704
  4.3 0.0 copy-start.3
  4.3 0.8 %copy-done.3 = bf16[1,160,128]{2,1,0:T(8,128)(2,1)S(1)} copy-done((bf16[1,160,128]{2,1,0:T(8,128)(2,1)S(1)}, bf16[1,160,128]{2,1,0:T(8,128)(2,1)}, u32[]{:S(2)}) %copy-start.3) | copy-done | bytes 40984
  5.1 0.0 copy-start.4
  5.1 0.8 %copy-done.4 = bf16[1,160,128]{2,1,0:T(8,128)(2,1)S(1)} copy-done((bf16[1,160,128]{2,1,0:T(8,128)(2,1)S(1)}, bf16[1,160,128]{2,1,0:T(8,128)(2,1)}, u32[]{:S(2)}) %copy-start.4) | copy-done | bytes 40984
  5.9 0.0 copy-start.5
  5.9 0.7 %copy-done.5 = s32[1,8]{1,0:T(1,128)S(1)} copy-done((s32[1,8]{1,0:T(1,128)S(1)}, s32[1,8]{1,0:T(1,128)}, u32[]{:S(2)}) %copy-start.5) | copy-done | bytes 56
  6.5 0.0 copy-start.6
  6.5 0.7 %copy-done.6 = s32[8]{0:T(128)S(1)} copy-done((s32[8]{0:T(128)S(1)}, s32[8]{0:T(128)}, u32[]{:S(2)}) %copy-start.6) | copy-done | bytes 56
  7.2 44.8 %shard_map.86 = (bf16[160,1024]{1,0:T(8,128)(2,1)S(1)}, bf16[256,256]{1,0:T(8,128)(2,1)S(1)}) custom-call(bf16[160,8192]{1,0:T(8,128)(2,1)S(1)} %bitcast.6, bf16[160,1024]{1,0:T(8,128)(2,1)S(1)} %bitcast.7, bf16[160,128]{1,0:T(8,128)(2,1)S(1)} %bitcast.10, bf16[160,128]{1,0:T(8,128)(2,1)S(1)} %bitcast.11, bf16[160,1024]{1,0:T(8,128)(2,1)S(1)} %bitcast.8, ...), custom_call_target="tpu_custom_call" | custom-call | tf_op jit(solution)/shard_map/pallas_call | solution.py:392
  52.0 0.7 %copy.11 = bf16[1,160,1024]{2,1,0:T(8,128)(2,1)} copy(bf16[1,160,1024]{2,1,0:T(8,128)(2,1)S(1)} %bitcast.9) | data formatting | bytes 655360
  52.8 0.7 %copy.12 = bf16[256,256]{1,0:T(8,128)(2,1)} copy(bf16[256,256]{1,0:T(8,128)(2,1)S(1)} %get-tuple-element.9) | data formatting | bytes 262144
Async XLA Ops:
  0.6 1.7 %copy-start = (bf16[1,160,8192]{2,1,0:T(8,128)(2,1)S(1)}, bf16[1,160,8192]{2,1,0:T(8,128)(2,1)}, u32[]{:S(2)}) copy-start(bf16[1,160,8192]{2,1,0:T(8,128)(2,1)} %param.7) | copy-start | bytes 7864324
  2.4 1.0 %copy-start.1 = (bf16[1,160,1024]{2,1,0:T(8,128)(2,1)S(1)}, bf16[1,160,1024]{2,1,0:T(8,128)(2,1)}, u32[]{:S(2)}) copy-start(bf16[1,160,1024]{2,1,0:T(8,128)(2,1)} %param.8) | copy-start | bytes 983044
  3.3 1.0 %copy-start.2 = (bf16[1,160,1024]{2,1,0:T(8,128)(2,1)S(1)}, bf16[1,160,1024]{2,1,0:T(8,128)(2,1)}, u32[]{:S(2)}) copy-start(bf16[1,160,1024]{2,1,0:T(8,128)(2,1)} %param.11) | copy-start | bytes 983044
  4.3 0.8 %copy-start.3 = (bf16[1,160,128]{2,1,0:T(8,128)(2,1)S(1)}, bf16[1,160,128]{2,1,0:T(8,128)(2,1)}, u32[]{:S(2)}) copy-start(bf16[1,160,128]{2,1,0:T(8,128)(2,1)} %param.9) | copy-start | bytes 122884
  5.1 0.8 %copy-start.4 = (bf16[1,160,128]{2,1,0:T(8,128)(2,1)S(1)}, bf16[1,160,128]{2,1,0:T(8,128)(2,1)}, u32[]{:S(2)}) copy-start(bf16[1,160,128]{2,1,0:T(8,128)(2,1)} %param.10) | copy-start | bytes 122884
  5.9 0.7 %copy-start.5 = (s32[1,8]{1,0:T(1,128)S(1)}, s32[1,8]{1,0:T(1,128)}, u32[]{:S(2)}) copy-start(s32[1,8]{1,0:T(1,128)} %refs_5_.1) | copy-start | bytes 100
  6.5 0.7 %copy-start.6 = (s32[8]{0:T(128)S(1)}, s32[8]{0:T(128)}, u32[]{:S(2)}) copy-start(s32[8]{0:T(128)} %refs_6_.1) | copy-start | bytes 100

commit v2 on v1

--- a/solution.py
+++ b/solution.py
@@ -143,8 +143,8 @@
 
 
 def kernel(
-    grad_scale, x_ref, q_ref, k_ref, v_ref, g_ref, len_ref, order_ref, dq_ref, dw_ref,
-    qs, gs, kbuf, vbuf, probs, dprobs, dscores, part, landed, pair, xa, xb,
+    grad_scale, x_ref, q_ref, k_ref, v_ref, g_ref, len_hbm, order_hbm, dq_ref, dw_ref,
+    len_ref, order_ref, load_sem, qs, gs, kbuf, vbuf, probs, dprobs, dscores, part, landed, pair, xa, xb,
     early, cross, crossed, zsum, zout, zland,
     k_send, k_recv, v_send, v_recv, x_send, x_recv, own_sem, part_send, part_recv,
     pair_send, pair_recv, cross_send, cross_recv, z_send, z_recv,
@@ -177,11 +177,15 @@
     for where in peers + close:
         pl.semaphore_signal(barrier, inc=1, device_id=where, device_id_type=pl.DeviceIdType.MESH)
 
-    for h in range(heads):
-        qs[h * rows:(h + 1) * rows, :] = q_ref[:, h * width:(h + 1) * width]
-        gs[h * rows:(h + 1) * rows, :] = g_ref[:, h * width:(h + 1) * width]
-    kbuf[0] = k_ref[...]
-    vbuf[0] = v_ref[...]
+    loads = [
+        (order_hbm, order_ref), (len_hbm, len_ref), (k_ref, kbuf.at[0]), (v_ref, vbuf.at[0]),
+    ]
+    for source, target in ((q_ref, qs), (g_ref, gs)):
+        for h in range(heads):
+            loads.append((source.at[:, pl.ds(h * width, width)], target.at[pl.ds(h * rows, rows), :]))
+    loads = [pltpu.make_async_copy(a, b, load_sem.at[n]) for n, (a, b) in enumerate(loads)]
+    for copy in loads:
+        copy.start()
 
     pl.semaphore_wait(barrier, len(peers) + len(close))
 
@@ -190,9 +194,8 @@
         where = peers[s - 1]
         kcopies.append(remote(k_ref, kbuf.at[s], k_send.at[s], k_recv.at[s], where))
         vcopies.append(remote(v_ref, vbuf.at[s], v_send.at[s], v_recv.at[s], where))
-    for s in (2, 1, 3):
+    for s in (1, 3, 2):
         kcopies[s].start()
-    for s in (2, 1, 3):
         vcopies[s].start()
     sent += kcopies[1:] + vcopies[1:]
 
@@ -221,6 +224,9 @@
         copy.start()
     sent += xcopies
 
+    for copy in loads[:2]:
+        copy.wait()
+
     lane = lax.broadcasted_iota(jnp.int32, (1, lanes), 1)
     inside = lane
     for h in range(1, heads):
@@ -244,31 +250,30 @@
     scale = width ** (-0.5)
     base2 = scale * math.log2(math.e)
     order = (0, 1, 3, 2)
-    best = None
+    for copy in loads[2:]:
+        copy.wait()
+    tops, sums, dots = {}, {}, {}
     for s in order:
         if s:
             kcopies[s].wait_recv()
+            vcopies[s].wait_recv()
         owner = (me - s + parts) % parts
         one = (order_ref[2 * owner]) * half
         two = (order_ref[2 * owner + 1] - 1) * half
         kpos = row + jnp.where(row < half, one, two)
         allowed = (kpos >= begin) & (kpos <= qpos)
         scores = jnp.where(allowed, nt(kbuf[s], qs[...]) * base2, -1e30)
-        probs[s] = scores
-        top = jnp.max(scores, axis=0, keepdims=True)
-        best = top if best is None else jnp.maximum(best, top)
-    total, weighted = 0.0, 0.0
-    for s in order:
-        if s:
-            vcopies[s].wait_recv()
-        prob = jnp.exp2(probs[s] - best)
+        tops[s] = jnp.max(scores, axis=0, keepdims=True)
+        prob = jnp.exp2(scores - tops[s])
         dprob = nt(vbuf[s], gs[...])
         probs[s] = prob
         dprobs[s] = dprob
-        total = total + jnp.sum(prob, axis=0, keepdims=True)
-        weighted = weighted + jnp.sum(prob * dprob, axis=0, keepdims=True)
-    inverse = 1.0 / total
-    delta = weighted * inverse
+        sums[s] = jnp.sum(prob, axis=0, keepdims=True)
+        dots[s] = jnp.sum(prob * dprob, axis=0, keepdims=True)
+    best = jnp.maximum(jnp.maximum(tops[0], tops[1]), jnp.maximum(tops[2], tops[3]))
+    gains = {s: jnp.exp2(tops[s] - best) for s in order}
+    inverse = 1.0 / sum(sums[s] * gains[s] for s in order)
+    delta = sum(dots[s] * gains[s] for s in order) * inverse
 
     partcopies = [None]
     for s in range(1, parts):
@@ -276,7 +281,7 @@
         partcopies.append(remote(part.at[s], landed.at[s], part_send.at[s], part_recv.at[s], where))
     own_pair = None
     for s in (2, 1, 3, 0):
-        prob = probs[s] * inverse
+        prob = probs[s] * (gains[s] * inverse)
         dscore = (prob * (dprobs[s] - delta)).astype(jnp.bfloat16)
         dscores[s * rows:(s + 1) * rows, :] = dscore
         dkey = nn(dscore, qs[...])
@@ -383,7 +388,6 @@
     grad_scale = (count * rows * parts) ** (-0.5)
     low, full = jnp.bfloat16, jnp.float32
     vmem = pl.BlockSpec(memory_space=pltpu.VMEM)
-    smem = pl.BlockSpec(memory_space=pltpu.SMEM)
     dma = pltpu.SemaphoreType.DMA
 
     def body(*refs):
@@ -395,9 +399,12 @@
             jax.ShapeDtypeStruct((rows, heads * width), low),
             jax.ShapeDtypeStruct((chunk, 2 * width), low),
         ),
-        in_specs=[pl.BlockSpec(memory_space=pl.ANY), vmem, vmem, vmem, vmem, smem, smem],
+        in_specs=[pl.BlockSpec(memory_space=pltpu.HBM)] * 7,
         out_specs=(vmem, vmem),
         scratch_shapes=[
+            pltpu.SMEM(doc_lengths.shape, jnp.int32),
+            pltpu.SMEM(block_order.shape, jnp.int32),
+            dma((4 + 2 * heads,)),
             pltpu.VMEM((lanes, width), low),
             pltpu.VMEM((lanes, width), low),
             pltpu.VMEM((parts, rows, width), low),
@@ -422,7 +429,7 @@
             dma((2, 2)), dma((2, 2)), dma((4,)), dma((4,)),
         ],
         compiler_params=pltpu.CompilerParams(
-            collective_id=0, has_side_effects=True, vmem_limit_bytes=48 * 1024 * 1024
+            collective_id=0, has_side_effects=True, vmem_limit_bytes=60 * 1024 * 1024
         ),
     )(layer_input[0], query_rows[0], key_rows[0], value_rows[0], grad_out[0], doc_lengths, block_order)
     return (query_grad[None], weight_grad)

time: 53.8 us -> 48.5 us (0.901)
  local copies, waits for them, and re-layouts: 7.92 us -> 3.29 us
    unnamed x16 -> x2, local copies, waits for them, and re-layouts: 7.92 us -> 3.29 us
where the time goes in v2:
time: 48.5 us; the launch traced here: 48.3 us
  Pallas kernels  44.3 us (91%)
  local copies, waits for them, and re-layouts  3.29 us (7%)
  between operations  0.64 us (1%)
    pallas_call x1, Pallas kernels, fused(): pl.pallas_call(body, out_shape=(jax.ShapeDtypeStruct((rows, heads * width...  44.3 us
    unnamed x2, local copies, waits for them, and re-layouts  3.29 us

profile of v2, /device:TPU:24, one launch (start us, length us, event | category | flops | bytes accessed | tf_op | source)
XLA Modules:
  0.0 48.3 jit_solution(10634177905068934837)
XLA Ops:
  0.6 44.3 %shard_map.86 = (bf16[160,1024]{1,0:T(8,128)(2,1)}, bf16[256,256]{1,0:T(8,128)(2,1)}) custom-call(bf16[160,8192]{1,0:T(8,128)(2,1)} %bitcast.6, bf16[160,1024]{1,0:T(8,128)(2,1)} %bitcast.7, bf16[160,128]{1,0:T(8,128)(2,1)} %bitcast.10, bf16[160,128]{1,0:T(8,128)(2,1)} %bitcast.11, bf16[160,1024]{1,0:T(8,128)(2,1)} %bitcast.8, s32[1,8]{1,0:T(1,128)} %refs_5_.1, ...), custom_call_target="tpu_custom_call" | custom-call | tf_op jit(solution)/shard_map/pallas_call | solution.py:396
  45.0 1.7 %copy.11 = bf16[1,160,1024]{2,1,0:T(8,128)(2,1)} copy(bf16[1,160,1024]{2,1,0:T(8,128)(2,1)} %bitcast.9) | data formatting | bytes 655360
  46.7 1.6 %copy.12 = bf16[256,256]{1,0:T(8,128)(2,1)} copy(bf16[256,256]{1,0:T(8,128)(2,1)} %get-tuple-element.9) | data formatting | bytes 262144

commit v3 on v2

--- a/solution.py
+++ b/solution.py
@@ -144,7 +144,7 @@
 
 def kernel(
     grad_scale, x_ref, q_ref, k_ref, v_ref, g_ref, len_hbm, order_hbm, dq_ref, dw_ref,
-    len_ref, order_ref, load_sem, qs, gs, kbuf, vbuf, probs, dprobs, dscores, part, landed, pair, xa, xb,
+    len_ref, order_ref, load_sem, qs, gs, kbuf, vbuf, probs, dprobs, dscores, part, landed, total_pair, pair, xa, xb,
     early, cross, crossed, zsum, zout, zland,
     k_send, k_recv, v_send, v_recv, x_send, x_recv, own_sem, part_send, part_recv,
     pair_send, pair_recv, cross_send, cross_recv, z_send, z_recv,
@@ -194,10 +194,22 @@
         where = peers[s - 1]
         kcopies.append(remote(k_ref, kbuf.at[s], k_send.at[s], k_recv.at[s], where))
         vcopies.append(remote(v_ref, vbuf.at[s], v_send.at[s], v_recv.at[s], where))
-    for s in (1, 3, 2):
-        kcopies[s].start()
-        vcopies[s].start()
-    sent += kcopies[1:] + vcopies[1:]
+    last = parts - 1
+    ends = (me == 0) | (me == last)
+    skipped = jnp.where(me == 0, last, 1)
+    kcopies[2].start()
+    vcopies[2].start()
+    for s in (1, 3):
+        @pl.when(jnp.logical_not(ends & (skipped == s)))
+        def _(s=s):
+            kcopies[s].start()
+            vcopies[s].start()
+    far = jnp.where(me == 1, 0, last)
+    relay_slot = jnp.where(me == 1, 1, last)
+    relays = [
+        remote(kbuf.at[2], kbuf.at[relay_slot], k_send.at[0], k_recv.at[relay_slot], (dp, far)),
+        remote(vbuf.at[2], vbuf.at[relay_slot], v_send.at[0], v_recv.at[relay_slot], (dp, far)),
+    ]
 
     xcopies, owned = [], []
     for slot, (cx, cc) in enumerate([(x, c), (x, 1 - c), (1 - x, c), (1 - x, 1 - c)]):
@@ -249,23 +261,44 @@
 
     scale = width ** (-0.5)
     base2 = scale * math.log2(math.e)
-    order = (0, 1, 3, 2)
     for copy in loads[2:]:
         copy.wait()
     tops, sums, dots = {}, {}, {}
-    for s in order:
-        if s:
-            kcopies[s].wait_recv()
-            vcopies[s].wait_recv()
-        owner = (me - s + parts) % parts
+    near_slot = jnp.where(me == 0, last, 1)
+    slots = [
+        0, jnp.where(ends, 2, 1), jnp.where(ends, near_slot, 2), jnp.where(ends, parts - near_slot, 3),
+    ]
+    order = range(parts)
+
+    def arrived(n):
+        to = (dp, (me + n) % parts)
+        remote(k_ref, kbuf.at[n], k_send.at[n], k_recv.at[n], to).wait_recv()
+        remote(v_ref, vbuf.at[n], v_send.at[n], v_recv.at[n], to).wait_recv()
+
+    for s, slot in enumerate(slots):
+        if s == 1:
+            arrived(2)
+
+            @pl.when(jnp.logical_not(ends))
+            def _():
+                for copy in relays:
+                    copy.start()
+                arrived(1)
+        elif s == 2:
+            @pl.when(ends)
+            def _():
+                arrived(near_slot)
+        elif s == 3:
+            arrived(slots[3])
+        owner = (me - slot + parts) % parts
         one = (order_ref[2 * owner]) * half
         two = (order_ref[2 * owner + 1] - 1) * half
         kpos = row + jnp.where(row < half, one, two)
         allowed = (kpos >= begin) & (kpos <= qpos)
-        scores = jnp.where(allowed, nt(kbuf[s], qs[...]) * base2, -1e30)
+        scores = jnp.where(allowed, nt(kbuf[slot], qs[...]) * base2, -1e30)
         tops[s] = jnp.max(scores, axis=0, keepdims=True)
         prob = jnp.exp2(scores - tops[s])
-        dprob = nt(vbuf[s], gs[...])
+        dprob = nt(vbuf[slot], gs[...])
         probs[s] = prob
         dprobs[s] = dprob
         sums[s] = jnp.sum(prob, axis=0, keepdims=True)
@@ -275,26 +308,49 @@
     inverse = 1.0 / sum(sums[s] * gains[s] for s in order)
     delta = sum(dots[s] * gains[s] for s in order) * inverse
 
-    partcopies = [None]
-    for s in range(1, parts):
-        where = (dp, (me - s + parts) % parts)
-        partcopies.append(remote(part.at[s], landed.at[s], part_send.at[s], part_recv.at[s], where))
+    beside = jnp.where(me == 0, 1, 2)
+    routes = {
+        3: (jnp.where(ends, beside, (me + 1) % parts), jnp.where(ends, 0, 3)),
+        1: ((me - slots[1] + parts) % parts, slots[1]),
+        2: ((me - slots[2] + parts) % parts, slots[2]),
+    }
+    partcopies = {
+        p: remote(part.at[p], landed.at[to], part_send.at[p], part_recv.at[to], (dp, device))
+        for p, (device, to) in routes.items()
+    }
+    handed = remote(part.at[3], landed.at[0], part_send.at[3], part_recv.at[0], (dp, beside))
+
+    @pl.when(ends)
+    def _():
+        landed[near_slot] = jnp.zeros(landed.shape[1:], landed.dtype)
+
     own_pair = None
-    for s in (2, 1, 3, 0):
+    for s in (3, 1, 2, 0):
         prob = probs[s] * (gains[s] * inverse)
         dscore = (prob * (dprobs[s] - delta)).astype(jnp.bfloat16)
         dscores[s * rows:(s + 1) * rows, :] = dscore
         dkey = nn(dscore, qs[...])
         dvalue = nn(prob.astype(jnp.bfloat16), gs[...])
-        if s:
+        if s in (3, 1):
             part[s, :, :width] = dkey.astype(jnp.bfloat16)
             part[s, :, width:] = dvalue.astype(jnp.bfloat16)
             partcopies[s].start()
+        elif s == 2:
+            total_pair[:, :width] = dkey
+            total_pair[:, width:] = dvalue
+
+            @pl.when(jnp.logical_not(ends))
+            def _():
+                handed.wait_recv()
+                total_pair[...] += landed[0].astype(jnp.float32)
+
+            part[2] = total_pair[...].astype(jnp.bfloat16)
+            partcopies[2].start()
         else:
             own_pair = (dkey, dvalue)
-    sent += partcopies[1:]
-
-    keys = kbuf[...].reshape(parts * rows, width)
+    sent += list(partcopies.values())
+
+    keys = jnp.concatenate([kbuf[slot] for slot in slots], axis=0)
     dquery = nn(keys.T, dscores[...]) * scale
     for h in range(heads):
         dq_ref[:, h * width:(h + 1) * width] = (
@@ -302,8 +358,13 @@
         )
 
     dkey, dvalue = own_pair
+    def part_in(n):
+        remote(part.at[n], landed.at[n], part_send.at[n], part_recv.at[n], (dp, (me + n) % parts)).wait_recv()
+
+    pl.when(me != last)(lambda: part_in(1))
+    pl.when(me != 0)(lambda: part_in(3))
+    part_in(2)
     for s in (1, 3, 2):
-        partcopies[s].wait_recv()
         dkey = dkey + landed[s, :, :width].astype(jnp.float32)
         dvalue = dvalue + landed[s, :, width:].astype(jnp.float32)
     pair[0:rows, :width] = (dkey * scale).astype(jnp.bfloat16)
@@ -374,6 +435,19 @@
         final = final + zland[s].astype(jnp.float32)
         sent.append(copy)
     dw_ref[...] = (final * grad_scale).T.astype(jnp.bfloat16)
+    kcopies[2].wait_send()
+    vcopies[2].wait_send()
+    for s in (1, 3):
+        @pl.when(jnp.logical_not(ends & (skipped == s)))
+        def _(s=s):
+            kcopies[s].wait_send()
+            vcopies[s].wait_send()
+
+    @pl.when(jnp.logical_not(ends))
+    def _():
+        for copy in relays:
+            copy.wait_send()
+
     for copy in sent:
         copy.wait_send()
 
@@ -414,6 +488,7 @@
             pltpu.VMEM((parts * rows, lanes), low),
             pltpu.VMEM((parts, rows, 2 * width), low),
             pltpu.VMEM((parts, rows, 2 * width), low),
+            pltpu.VMEM((rows, 2 * width), full),
             pltpu.VMEM((6 * rows, 2 * width), low),
             pltpu.VMEM((2, 4 * rows, 2 * chunk), low),
             pltpu.VMEM((2, 4 * rows, 2 * chunk), low),

time: 48.5 us -> 47.4 us (0.977)
  the two profiles are of different devices: /device:TPU:24 before, /device:TPU:0 now
where the time goes in v3:
time: 47.4 us; the launch traced here: 47.2 us
  Pallas kernels  43.3 us (91%)
  local copies, waits for them, and re-layouts  3.29 us (7%)
  between operations  0.64 us (1%)
    pallas_call x1, Pallas kernels, fused(): pl.pallas_call(body, out_shape=(jax.ShapeDtypeStruct((rows, heads * width...  43.3 us
    unnamed x2, local copies, waits for them, and re-layouts  3.29 us

profile of v3, /device:TPU:0, one launch (start us, length us, event | category | flops | bytes accessed | tf_op | source)
XLA Modules:
  0.0 47.2 jit_solution(6937344122440204385)
XLA Ops:
  0.6 43.3 %shard_map.86 = (bf16[160,1024]{1,0:T(8,128)(2,1)}, bf16[256,256]{1,0:T(8,128)(2,1)}) custom-call(bf16[160,8192]{1,0:T(8,128)(2,1)} %bitcast.6, bf16[160,1024]{1,0:T(8,128)(2,1)} %bitcast.7, bf16[160,128]{1,0:T(8,128)(2,1)} %bitcast.10, bf16[160,128]{1,0:T(8,128)(2,1)} %bitcast.11, bf16[160,1024]{1,0:T(8,128)(2,1)} %bitcast.8, s32[1,8]{1,0:T(1,128)} %refs_5_.1, ...), custom_call_target="tpu_custom_call" | custom-call | tf_op jit(solution)/shard_map/pallas_call | solution.py:470
  43.9 1.7 %copy.11 = bf16[1,160,1024]{2,1,0:T(8,128)(2,1)} copy(bf16[1,160,1024]{2,1,0:T(8,128)(2,1)} %bitcast.9) | data formatting | bytes 655360
  45.6 1.6 %copy.12 = bf16[256,256]{1,0:T(8,128)(2,1)} copy(bf16[256,256]{1,0:T(8,128)(2,1)} %get-tuple-element.9) | data formatting | bytes 262144

commit v4 on v2

--- a/solution.py
+++ b/solution.py
@@ -144,7 +144,7 @@
 
 def kernel(
     grad_scale, x_ref, q_ref, k_ref, v_ref, g_ref, len_hbm, order_hbm, dq_ref, dw_ref,
-    len_ref, order_ref, load_sem, qs, gs, kbuf, vbuf, probs, dprobs, dscores, part, landed, pair, xa, xb,
+    len_ref, order_ref, load_sem, qs, gs, kbuf, vbuf, probs, dprobs, dscores, part, landed, pair, xab, turned,
     early, cross, crossed, zsum, zout, zland,
     k_send, k_recv, v_send, v_recv, x_send, x_recv, own_sem, part_send, part_recv,
     pair_send, pair_recv, cross_send, cross_recv, z_send, z_recv,
@@ -204,7 +204,7 @@
         for t in range(2):
             first = pl.multiple_of(place(t, cx, cc) * (parts * chunk), parts * chunk)
             source = x_ref.at[:, pl.ds(first, 2 * chunk)]
-            target = xa.at[t, pl.ds(slot * rows, rows), :]
+            target = xab.at[0, t, pl.ds(slot * rows, rows), :]
             if slot == 0:
                 owned.append(pltpu.make_async_copy(source, target, own_sem.at[t]))
             else:
@@ -214,7 +214,7 @@
         for t in range(2):
             first = pl.multiple_of(place(cy, t, cc) * (parts * chunk) + 2 * chunk, 2 * chunk)
             source = x_ref.at[:, pl.ds(first, 2 * chunk)]
-            target = xb.at[t, pl.ds(slot * rows, rows), :]
+            target = xab.at[1, t, pl.ds(slot * rows, rows), :]
             if slot == 0:
                 owned.append(pltpu.make_async_copy(source, target, own_sem.at[2 + t]))
             else:
@@ -324,55 +324,90 @@
     for copy in xcopies:
         copy.wait_recv()
     paircopies[1].wait_recv()
-    turned = pair[0:2 * rows, :].T
-    for t in range(2):
-        early[0, t] = nn(turned, xa[t, 0:2 * rows, :])
-        early[1, t] = nn(turned, xb[t, 0:2 * rows, :])
-    crosscopies = [[], []]
+    last = parts - 1
+    ends = (me == 0) | (me == last)
+    beside = jnp.where(me == 0, 1, 2)
+    first_turned = pair[0:2 * rows, :].T
+    columns = [slice(z * chunk, (z + 1) * chunk) for z in range(2)]
+    for a in range(2):
+        for t in range(2):
+            for z in range(2):
+                early[a, t, z] = nn(first_turned, xab[a, t, 0:2 * rows, columns[z]])
     kept = (y, x)
-    away = [(place(1 - y, x, c), me), (place(y, 1 - x, c), me)]
+    away = (place(1 - y, x, c), place(y, 1 - x, c))
+    goals = [
+        jnp.where((me == 0) | (me == 2), 3, 0),
+        jnp.where(me % 2 == 0, 1, 2),
+        jnp.where(ends, jnp.where(me == 0, 2, 1), jnp.where(me == 1, 3, 0)),
+        me,
+    ]
+    halves = [pl.ds(h * width, width) for h in range(2)]
+
+    @pl.when(ends)
+    def _():
+        zland[jnp.where(me == 0, 1, 3)] = jnp.zeros(zland.shape[1:], zland.dtype)
+
+    for n in (2, 3, 4, 5):
+        paircopies[n].wait_recv()
+    for a in range(2):
+        turned[a] = pair[(2 + 2 * a) * rows:(4 + 2 * a) * rows, :].T
+    crosscopies = []
+    for k, goal in enumerate(goals):
+        a, z = goal // 2, goal % 2
+        other = 1 - jnp.where(a == 0, y, x)
+        late = xab[a, other, pl.ds(2 * rows, 2 * rows), pl.ds(pl.multiple_of(z * chunk, chunk), chunk)]
+        cross[k] = (early[a, other, z] + nn(turned[a], late)).astype(jnp.bfloat16)
+        where = (jnp.where(a == 0, away[0], away[1]), me)
+        for h in range(2):
+            copy = remote(
+                cross.at[k, halves[h], :], crossed.at[k, halves[h], :],
+                cross_send.at[k, h], cross_recv.at[k, h], where,
+            )
+            copy.start()
+            crosscopies.append(copy)
     for a in range(2):
         for z in range(2):
-            crosscopies[a].append(remote(
-                cross.at[a, z], crossed.at[a, z], cross_send.at[a, z], cross_recv.at[a, z], away[a],
-            ))
-    turns = []
-    for a, xs in enumerate((xa, xb)):
-        paircopies[2 + 2 * a].wait_recv()
-        paircopies[3 + 2 * a].wait_recv()
-        turned = pair[(2 + 2 * a) * rows:(4 + 2 * a) * rows, :].T
-        turns.append(turned)
-        other = 1 - kept[a]
-        for z in range(2):
-            cols = slice(z * chunk, (z + 1) * chunk)
-            made = early[a, other, :, cols] + nn(turned, xs[other, 2 * rows:4 * rows, cols])
-            cross[a, z] = made.astype(jnp.bfloat16)
-            crosscopies[a][z].start()
-    for a, xs in enumerate((xa, xb)):
-        for z in range(2):
-            cols = slice(z * chunk, (z + 1) * chunk)
-            zsum[2 * a + z] = early[a, kept[a], :, cols] + nn(turns[a], xs[kept[a], 2 * rows:4 * rows, cols])
-        sent += crosscopies[a]
-
-    for z, a in ((0, 0), (1, 0), (0, 1), (1, 1)):
-        t = 2 * a + z
-        crosscopies[a][z].wait_recv()
-        made = zsum[t] + crossed[a, z].astype(jnp.float32)
-        zsum[t] = made
-        zout[t] = made.astype(jnp.bfloat16)
-
-        @pl.when(me != t)
-        def _():
-            s = (t - me + parts) % parts
-            remote(zout.at[t], zland.at[s], z_send.at[s], z_recv.at[s], (dp, t)).start()
-
+            late = xab[a, kept[a], 2 * rows:4 * rows, columns[z]]
+            zsum[2 * a + z] = early[a, kept[a], z] + nn(turned[a], late)
+    sent += crosscopies
+
+    for k, goal in enumerate(goals):
+        device, to = goal, (goal - me + parts) % parts
+        if k == 0:
+            device, to = jnp.where(ends, beside, device), jnp.where(ends, 0, to)
+        for h in range(2):
+            crosscopies[2 * k + h].wait_recv()
+            zsum[goal, halves[h], :] += crossed[k, halves[h], :].astype(jnp.float32)
+            if k == 2:
+                @pl.when(jnp.logical_not(ends))
+                def _():
+                    remote(
+                        zout.at[0, halves[h], :], zland.at[0, halves[h], :],
+                        z_send.at[0, h], z_recv.at[0, h], (dp, beside),
+                    ).wait_recv()
+                    zsum[goal, halves[h], :] += zland[0, halves[h], :].astype(jnp.float32)
+            if k < 3:
+                zout[k, halves[h], :] = zsum[goal, halves[h], :].astype(jnp.bfloat16)
+                copy = remote(
+                    zout.at[k, halves[h], :], zland.at[to, halves[h], :],
+                    z_send.at[k, h], z_recv.at[to, h], (dp, device),
+                )
+                copy.start()
+                sent.append(copy)
+
+    def sum_in(n):
+        for h in range(2):
+            remote(
+                zout.at[0, halves[h], :], zland.at[n, halves[h], :],
+                z_send.at[0, h], z_recv.at[n, h], (dp, (me + n) % parts),
+            ).wait_recv()
+
+    pl.when(me != 0)(lambda: sum_in(1))
+    pl.when(me != last)(lambda: sum_in(3))
+    sum_in(2)
     final = zsum[me]
     for s in (1, 3, 2):
-        to = (me + s) % parts
-        copy = remote(zout.at[to], zland.at[s], z_send.at[s], z_recv.at[s], (dp, to))
-        copy.wait_recv()
         final = final + zland[s].astype(jnp.float32)
-        sent.append(copy)
     dw_ref[...] = (final * grad_scale).T.astype(jnp.bfloat16)
     for copy in sent:
         copy.wait_send()
@@ -415,18 +450,18 @@
             pltpu.VMEM((parts, rows, 2 * width), low),
             pltpu.VMEM((parts, rows, 2 * width), low),
             pltpu.VMEM((6 * rows, 2 * width), low),
-            pltpu.VMEM((2, 4 * rows, 2 * chunk), low),
-            pltpu.VMEM((2, 4 * rows, 2 * chunk), low),
-            pltpu.VMEM((2, 2, 2 * width, 2 * chunk), full),
-            pltpu.VMEM((2, 2, 2 * width, chunk), low),
-            pltpu.VMEM((2, 2, 2 * width, chunk), low),
+            pltpu.VMEM((2, 2, 4 * rows, 2 * chunk), low),
+            pltpu.VMEM((2, 2 * width, 2 * rows), low),
+            pltpu.VMEM((2, 2, 2, 2 * width, chunk), full),
+            pltpu.VMEM((4, 2 * width, chunk), low),
+            pltpu.VMEM((4, 2 * width, chunk), low),
             pltpu.VMEM((4, 2 * width, chunk), full),
             pltpu.VMEM((4, 2 * width, chunk), low),
             pltpu.VMEM((4, 2 * width, chunk), low),
             dma((4,)), dma((4,)), dma((4,)), dma((4,)),
             dma((2, 8)), dma((2, 8)), dma((4,)),
             dma((4,)), dma((4,)), dma((6,)), dma((6,)),
-            dma((2, 2)), dma((2, 2)), dma((4,)), dma((4,)),
+            dma((4, 2)), dma((4, 2)), dma((4, 2)), dma((4, 2)),
         ],
         compiler_params=pltpu.CompilerParams(
             collective_id=0, has_side_effects=True, vmem_limit_bytes=60 * 1024 * 1024

time: 48.5 us -> 47.2 us (0.973)
  the two profiles are of different devices: /device:TPU:24 before, /device:TPU:0 now
where the time goes in v4:
time: 47.2 us; the launch traced here: 47 us
  Pallas kernels  43.1 us (91%)
  local copies, waits for them, and re-layouts  3.29 us (7%)
  between operations  0.64 us (1%)
    pallas_call x1, Pallas kernels, fused(): pl.pallas_call(body, out_shape=(jax.ShapeDtypeStruct((rows, heads * width...  43.1 us
    unnamed x2, local copies, waits for them, and re-layouts  3.29 us

profile of v4, /device:TPU:0, one launch (start us, length us, event | category | flops | bytes accessed | tf_op | source)
XLA Modules:
  0.0 47.0 jit_solution(8004270893561303428)
XLA Ops:
  0.6 43.1 %shard_map.86 = (bf16[160,1024]{1,0:T(8,128)(2,1)}, bf16[256,256]{1,0:T(8,128)(2,1)}) custom-call(bf16[160,8192]{1,0:T(8,128)(2,1)} %bitcast.6, bf16[160,1024]{1,0:T(8,128)(2,1)} %bitcast.7, bf16[160,128]{1,0:T(8,128)(2,1)} %bitcast.10, bf16[160,128]{1,0:T(8,128)(2,1)} %bitcast.11, bf16[160,1024]{1,0:T(8,128)(2,1)} %bitcast.8, s32[1,8]{1,0:T(1,128)} %refs_5_.1, ...), custom_call_target="tpu_custom_call" | custom-call | tf_op jit(solution)/shard_map/pallas_call | solution.py:431
  43.8 1.7 %copy.11 = bf16[1,160,1024]{2,1,0:T(8,128)(2,1)} copy(bf16[1,160,1024]{2,1,0:T(8,128)(2,1)} %bitcast.9) | data formatting | bytes 655360
  45.5 1.6 %copy.12 = bf16[256,256]{1,0:T(8,128)(2,1)} copy(bf16[256,256]{1,0:T(8,128)(2,1)} %get-tuple-element.9) | data formatting | bytes 262144
